TPU v7x, 32 devices: a whole 2x2x4 slice. The times are simulated.
32 devices in a mesh: lev: 2 (over x), gx: 8 (over z, y), gy: 2 (over core).
Axes of the slice: x: 2, y: 2, z: 4, core: 2. Of those that a mesh axis runs over, the one named last changes fastest.
Arguments:
- increments: float32 [1, 2, 80, 128, 256], P(None, None, 'lev', 'gx', 'gy'), may hold values from -6 to 6
- vert_corr: float32 [2, 80, 80], replicated, may hold values from -0.025 to 1, as said below
- kappa: float32 [2, 128, 256], P(None, 'gx', 'gy'), may hold values from 0.03 to 0.24
- sea_mask: int32 [80, 128, 256], P('lev', 'gx', 'gy'), may hold values 0 or 1
- level_count: int32 [128, 256], P('gx', 'gy'), may hold values from 10 to 75
Outputs:
- covaried: float32 [1, 2, 80, 128, 256], P(None, None, 'lev', 'gx', 'gy')
Inputs may be any that keep to these rules, and one draw needn't show every extreme that they name: vert_corr has ones on the diagonal, and each row's other entries together have magnitude below one.
All inputs are finite; a program needn't handle non-finite values. No bound on the sum of `sea_mask` on one device may be relied on, other than what follows from the above.
Results may differ from a plain program's by a relative error of at most 0.00021.
Values sent between devices are 32-bit elements; how exact they have to be, the bound alone decides.
A program may use at most 64 MiB of HBM per device.

v0:
```python
import jax
import jax.numpy as jnp
from jax import lax
from jax.sharding import PartitionSpec as P

PASSES = 10


def from_behind(block, axis, distance):
    devices = range(lax.axis_size(axis))
    route = [((i - distance) % len(devices), i) for i in devices]
    return lax.ppermute(block, axis, route)


def shifted(block, axis, distance):
    devices = range(lax.axis_size(axis))
    route = [(i - distance, i) for i in devices if i - distance in devices]
    return lax.ppermute(block, axis, route)


def padded(cells, sides, width):
    for axis, dim in sides:
        count = lax.axis_size(axis)
        head = lax.slice_in_dim(cells, 0, width, axis=dim)
        tail = lax.slice_in_dim(cells, cells.shape[dim] - width, cells.shape[dim], axis=dim)
        cells = jnp.concatenate(
            [
                lax.ppermute(tail, axis, [(i, (i + 1) % count) for i in range(count)]),
                cells,
                lax.ppermute(head, axis, [((i + 1) % count, i) for i in range(count)]),
            ],
            axis=dim,
        )
    return cells


def relax(extended, east_ext, north_ext, wet_center):
    center = extended[..., 1:-1, 1:-1]
    flux = east_ext[1:-1, 1:-1] * (extended[..., 2:, 1:-1] - center)
    flux = flux + east_ext[:-2, 1:-1] * (extended[..., :-2, 1:-1] - center)
    flux = flux + north_ext[1:-1, 1:-1] * (extended[..., 1:-1, 2:] - center)
    flux = flux + north_ext[1:-1, :-2] * (extended[..., 1:-1, :-2] - center)
    return wet_center * (center + flux)


def per_device(increments, vert_corr, kappa, sea_mask, level_count):
    lev_dev = sea_mask.shape[0]
    cells_x = sea_mask.shape[1]
    cells_y = sea_mask.shape[2]
    lev_first = lax.axis_index("lev") * lev_dev
    levels = lev_first + jnp.arange(lev_dev, dtype=jnp.int32)
    wet = sea_mask * (levels[:, None, None] < level_count[None]).astype(jnp.int32)
    wet_float = wet.astype(jnp.float32)
    masked = increments * wet_float
    own_rows = lax.dynamic_slice_in_dim(vert_corr, lev_first, lev_dev, 1)
    correlated = jnp.einsum(
        "toh,dthxy->dtoxy",
        own_rows,
        lax.all_gather(masked, "lev", axis=2, tiled=True),
        precision=lax.Precision.HIGHEST,
    )
    field = correlated * wet_float
    total_y = cells_y * lax.axis_size("gy")
    local_rows = lax.axis_index("gy") * cells_y + jnp.arange(cells_y, dtype=jnp.int32)
    open_local = (local_rows != total_y - 1).astype(jnp.float32)
    east_local = kappa[0]
    north_local = kappa[1] * open_local[None, :]
    east_low = from_behind(east_local[-1:, :], "gx", 1)
    north_low = shifted(north_local[:, -1:], "gy", 1)
    zero_row = jnp.zeros((1, cells_y), jnp.float32)
    zero_col = jnp.zeros((cells_x, 1), jnp.float32)
    east_ext = jnp.pad(jnp.concatenate([east_low, east_local, zero_row], axis=0), ((0, 0), (1, 1)))
    north_ext = jnp.pad(
        jnp.concatenate([north_low, north_local, zero_col], axis=1), ((1, 1), (0, 0))
    )

    def one_pass(step, current):
        extended = padded(current, (("gx", 3), ("gy", 4)), 1)
        return relax(extended, east_ext, north_ext, wet_float)

    field = lax.fori_loop(0, PASSES, one_pass, field)
    return field


def solution(mesh):
    in_specs = (
        P(None, None, "lev", "gx", "gy"),
        P(),
        P(None, "gx", "gy"),
        P("lev", "gx", "gy"),
        P("gx", "gy"),
    )
    out_specs = P(None, None, "lev", "gx", "gy")
    return jax.shard_map(
        per_device, mesh=mesh, in_specs=in_specs, out_specs=out_specs, check_vma=False
    )
```

profile of v0, /device:TPU:0, one launch (start us, length us, event | category | flops | bytes accessed | tf_op | source)
XLA Modules:
  0.0 171.8 jit_solution(11940098655885477659)
XLA Ops:
  7.7 2.1 %copy_multiply_fusion = f32[1,2,40,16,128]{4,2,3,1,0:T(8,128)} fusion(f32[1,2,40,16,128]{4,3,2,1,0:T(8,128)} %param.7, f32[40,16,128]{2,0,1:T(8,128)S(1)} %fusion.21), kind=kLoop, calls=%fused_computation.24 | loop fusion | flops 163840 | bytes 1638400 | tf_op jit(solution)/shard_map/mul | solution.py:54
  9.9 3.0 %collective-permute-start.4 = (f32[1,128]{1,0:T(1,128)S(1)}, f32[1,128]{1,0:T(1,128)S(1)}, u32[]{:S(2)}, u32[]{:S(2)}) collective-permute-start(f32[1,128]{1,0:T(1,128)S(1)} %slice_bitcast_fusion.1), channel_id=1, source_target_pairs={{14,0},{0,2},{2,4},{4,6},{6,8},{8,10},{10,12},{12,14},{15,1},{1,3}... | collective-permute-start | bytes 1544 | tf_op jit(solution)/shard_map/ppermute | solution.py:12
  15.3 2.1 %collective-permute-done.4 = f32[1,128]{1,0:T(1,128)S(1)} collective-permute-done((f32[1,128]{1,0:T(1,128)S(1)}, f32[1,128]{1,0:T(1,128)S(1)}, u32[]{:S(2)}, u32[]{:S(2)}) %collective-permute-start.4) | collective-permute-done | bytes 544 | tf_op jit(solution)/shard_map/ppermute | solution.py:12
  17.6 19.4 %all-gather.2.cloned.1.call-done = f32[1,2,80,16,128]{4,2,3,1,0:T(8,128)} async-done(((f32[1,2,40,16,128]{4,2,3,1,0:T(8,128)}), f32[1,2,80,16,128]{4,2,3,1,0:T(8,128)}) %all-gather.2.cloned.1.call-update) | async-done | bytes 1310736 | tf_op jit(solution)/shard_map/all_gather | solution.py:59
  37.0 3.0 %fusion.18 = f32[1,2,40,16,128]{4,2,3,1,0:T(8,128)} fusion(f32[1,2,80,16,128]{4,2,3,1,0:T(8,128)} %all-gather.2.cloned.1.call-done, f32[40,16,128]{2,0,1:T(8,128)S(1)} %fusion.21, f32[2,80,80]{2,1,0:T(8,128)S(1)} %copy-done, s32[]{:T(128)S(6)} %select_n.3), kind=kOutput, calls=%fused_computation.23 | convolution fusion | flops 157450240 | bytes 2334724 | tf_op jit(solution)/shard_map/toh,dthxy->dtoxy/dot_general | solution.py:56
  40.0 122.9 %while.10 = (s32[]{:T(128)}, f32[1,2,40,16,128]{4,2,3,1,0:T(8,128)}, f32[40,16,128]{2,0,1:T(8,128)S(1)}, f32[18,130]{1,0:T(8,128)S(1)}, f32[18,130]{1,0:T(8,128)S(1)}, /*index=5*/s32[]{:T(128)}) while((s32[]{:T(128)}, f32[1,2,40,16,128]{4,2,3,1,0:T(8,128)}, f32[40,16,128]{2,0,1:T(8,128)S(1)}, f32[18,130]{1,0:T(8,128)S(1)}, ...), condition=%wide.region_1.2_spmd, body=%wide.region_0.1_spmd.sunk | while | flops 2785282 | bytes 5959653 | solution.py:81
  41.1 1.5 collective-permute-start
  42.6 3.2 %collective-permute-start.1 = (f32[1,2,40,1,128]{4,2,3,1,0:T(8,128)S(1)}, f32[1,2,40,1,128]{4,2,3,1,0:T(8,128)S(1)}, u32[]{:S(2)}, u32[]{:S(2)}) collective-permute-start(f32[1,2,40,1,128]{4,2,3,1,0:T(8,128)S(1)} %get-tuple-element.103), channel_id=1, source_target_pairs={{2,0},{4,2},{6,4},{8,6},{10,8},{12,10},{14,12},{0,14},{3,1},{5,3},... | collective-permute-start | bytes 122888 | tf_op jit(solution)/shard_map/while/body/eval_jaxpr/ppermute | solution.py:30
  45.8 2.0 %collective-permute-done = f32[1,2,40,1,128]{4,2,3,1,0:T(8,128)S(1)} collective-permute-done((f32[1,2,40,1,128]{4,2,3,1,0:T(8,128)S(1)}, f32[1,2,40,1,128]{4,2,3,1,0:T(8,128)S(1)}, u32[]{:S(2)}, u32[]{:S(2)}) %collective-permute-start) | collective-permute-done | bytes 40992 | tf_op jit(solution)/shard_map/while/body/eval_jaxpr/ppermute | solution.py:28
  54.5 3.6 %collective-permute-start.1 = (f32[1,2,40,1,128]{4,2,3,1,0:T(8,128)S(1)}, f32[1,2,40,1,128]{4,2,3,1,0:T(8,128)S(1)}, u32[]{:S(2)}, u32[]{:S(2)}) collective-permute-start(f32[1,2,40,1,128]{4,2,3,1,0:T(8,128)S(1)} %get-tuple-element.103), channel_id=1, source_target_pairs={{2,0},{4,2},{6,4},{8,6},{10,8},{12,10},{14,12},{0,14},{3,1},{5,3},... | collective-permute-start | bytes 122888 | tf_op jit(solution)/shard_map/while/body/eval_jaxpr/ppermute | solution.py:30
  58.1 2.0 %collective-permute-done = f32[1,2,40,1,128]{4,2,3,1,0:T(8,128)S(1)} collective-permute-done((f32[1,2,40,1,128]{4,2,3,1,0:T(8,128)S(1)}, f32[1,2,40,1,128]{4,2,3,1,0:T(8,128)S(1)}, u32[]{:S(2)}, u32[]{:S(2)}) %collective-permute-start) | collective-permute-done | bytes 40992 | tf_op jit(solution)/shard_map/while/body/eval_jaxpr/ppermute | solution.py:28
  63.1 1.5 fusion.36
  65.7 4.7 %collective-permute-start.1 = (f32[1,2,40,1,128]{4,2,3,1,0:T(8,128)S(1)}, f32[1,2,40,1,128]{4,2,3,1,0:T(8,128)S(1)}, u32[]{:S(2)}, u32[]{:S(2)}) collective-permute-start(f32[1,2,40,1,128]{4,2,3,1,0:T(8,128)S(1)} %get-tuple-element.103), channel_id=1, source_target_pairs={{2,0},{4,2},{6,4},{8,6},{10,8},{12,10},{14,12},{0,14},{3,1},{5,3},... | collective-permute-start | bytes 122888 | tf_op jit(solution)/shard_map/while/body/eval_jaxpr/ppermute | solution.py:30
  70.4 2.0 %collective-permute-done = f32[1,2,40,1,128]{4,2,3,1,0:T(8,128)S(1)} collective-permute-done((f32[1,2,40,1,128]{4,2,3,1,0:T(8,128)S(1)}, f32[1,2,40,1,128]{4,2,3,1,0:T(8,128)S(1)}, u32[]{:S(2)}, u32[]{:S(2)}) %collective-permute-start) | collective-permute-done | bytes 40992 | tf_op jit(solution)/shard_map/while/body/eval_jaxpr/ppermute | solution.py:28
  75.4 1.5 fusion.36
  77.9 4.7 %collective-permute-start.1 = (f32[1,2,40,1,128]{4,2,3,1,0:T(8,128)S(1)}, f32[1,2,40,1,128]{4,2,3,1,0:T(8,128)S(1)}, u32[]{:S(2)}, u32[]{:S(2)}) collective-permute-start(f32[1,2,40,1,128]{4,2,3,1,0:T(8,128)S(1)} %get-tuple-element.103), channel_id=1, source_target_pairs={{2,0},{4,2},{6,4},{8,6},{10,8},{12,10},{14,12},{0,14},{3,1},{5,3},... | collective-permute-start | bytes 122888 | tf_op jit(solution)/shard_map/while/body/eval_jaxpr/ppermute | solution.py:30
  82.6 2.0 %collective-permute-done = f32[1,2,40,1,128]{4,2,3,1,0:T(8,128)S(1)} collective-permute-done((f32[1,2,40,1,128]{4,2,3,1,0:T(8,128)S(1)}, f32[1,2,40,1,128]{4,2,3,1,0:T(8,128)S(1)}, u32[]{:S(2)}, u32[]{:S(2)}) %collective-permute-start) | collective-permute-done | bytes 40992 | tf_op jit(solution)/shard_map/while/body/eval_jaxpr/ppermute | solution.py:28
  90.2 4.7 %collective-permute-start.1 = (f32[1,2,40,1,128]{4,2,3,1,0:T(8,128)S(1)}, f32[1,2,40,1,128]{4,2,3,1,0:T(8,128)S(1)}, u32[]{:S(2)}, u32[]{:S(2)}) collective-permute-start(f32[1,2,40,1,128]{4,2,3,1,0:T(8,128)S(1)} %get-tuple-element.103), channel_id=1, source_target_pairs={{2,0},{4,2},{6,4},{8,6},{10,8},{12,10},{14,12},{0,14},{3,1},{5,3},... | collective-permute-start | bytes 122888 | tf_op jit(solution)/shard_map/while/body/eval_jaxpr/ppermute | solution.py:30
  95.0 2.0 %collective-permute-done = f32[1,2,40,1,128]{4,2,3,1,0:T(8,128)S(1)} collective-permute-done((f32[1,2,40,1,128]{4,2,3,1,0:T(8,128)S(1)}, f32[1,2,40,1,128]{4,2,3,1,0:T(8,128)S(1)}, u32[]{:S(2)}, u32[]{:S(2)}) %collective-permute-start) | collective-permute-done | bytes 40992 | tf_op jit(solution)/shard_map/while/body/eval_jaxpr/ppermute | solution.py:28
  102.5 4.7 %collective-permute-start.1 = (f32[1,2,40,1,128]{4,2,3,1,0:T(8,128)S(1)}, f32[1,2,40,1,128]{4,2,3,1,0:T(8,128)S(1)}, u32[]{:S(2)}, u32[]{:S(2)}) collective-permute-start(f32[1,2,40,1,128]{4,2,3,1,0:T(8,128)S(1)} %get-tuple-element.103), channel_id=1, source_target_pairs={{2,0},{4,2},{6,4},{8,6},{10,8},{12,10},{14,12},{0,14},{3,1},{5,3},... | collective-permute-start | bytes 122888 | tf_op jit(solution)/shard_map/while/body/eval_jaxpr/ppermute | solution.py:30
  107.2 2.0 %collective-permute-done = f32[1,2,40,1,128]{4,2,3,1,0:T(8,128)S(1)} collective-permute-done((f32[1,2,40,1,128]{4,2,3,1,0:T(8,128)S(1)}, f32[1,2,40,1,128]{4,2,3,1,0:T(8,128)S(1)}, u32[]{:S(2)}, u32[]{:S(2)}) %collective-permute-start) | collective-permute-done | bytes 40992 | tf_op jit(solution)/shard_map/while/body/eval_jaxpr/ppermute | solution.py:28
  112.3 1.5 fusion.36
  114.8 4.7 %collective-permute-start.1 = (f32[1,2,40,1,128]{4,2,3,1,0:T(8,128)S(1)}, f32[1,2,40,1,128]{4,2,3,1,0:T(8,128)S(1)}, u32[]{:S(2)}, u32[]{:S(2)}) collective-permute-start(f32[1,2,40,1,128]{4,2,3,1,0:T(8,128)S(1)} %get-tuple-element.103), channel_id=1, source_target_pairs={{2,0},{4,2},{6,4},{8,6},{10,8},{12,10},{14,12},{0,14},{3,1},{5,3},... | collective-permute-start | bytes 122888 | tf_op jit(solution)/shard_map/while/body/eval_jaxpr/ppermute | solution.py:30
  119.5 2.0 %collective-permute-done = f32[1,2,40,1,128]{4,2,3,1,0:T(8,128)S(1)} collective-permute-done((f32[1,2,40,1,128]{4,2,3,1,0:T(8,128)S(1)}, f32[1,2,40,1,128]{4,2,3,1,0:T(8,128)S(1)}, u32[]{:S(2)}, u32[]{:S(2)}) %collective-permute-start) | collective-permute-done | bytes 40992 | tf_op jit(solution)/shard_map/while/body/eval_jaxpr/ppermute | solution.py:28
  124.5 1.5 fusion.36
  127.1 4.7 %collective-permute-start.1 = (f32[1,2,40,1,128]{4,2,3,1,0:T(8,128)S(1)}, f32[1,2,40,1,128]{4,2,3,1,0:T(8,128)S(1)}, u32[]{:S(2)}, u32[]{:S(2)}) collective-permute-start(f32[1,2,40,1,128]{4,2,3,1,0:T(8,128)S(1)} %get-tuple-element.103), channel_id=1, source_target_pairs={{2,0},{4,2},{6,4},{8,6},{10,8},{12,10},{14,12},{0,14},{3,1},{5,3},... | collective-permute-start | bytes 122888 | tf_op jit(solution)/shard_map/while/body/eval_jaxpr/ppermute | solution.py:30
  131.8 2.0 %collective-permute-done = f32[1,2,40,1,128]{4,2,3,1,0:T(8,128)S(1)} collective-permute-done((f32[1,2,40,1,128]{4,2,3,1,0:T(8,128)S(1)}, f32[1,2,40,1,128]{4,2,3,1,0:T(8,128)S(1)}, u32[]{:S(2)}, u32[]{:S(2)}) %collective-permute-start) | collective-permute-done | bytes 40992 | tf_op jit(solution)/shard_map/while/body/eval_jaxpr/ppermute | solution.py:28
  139.4 4.7 %collective-permute-start.1 = (f32[1,2,40,1,128]{4,2,3,1,0:T(8,128)S(1)}, f32[1,2,40,1,128]{4,2,3,1,0:T(8,128)S(1)}, u32[]{:S(2)}, u32[]{:S(2)}) collective-permute-start(f32[1,2,40,1,128]{4,2,3,1,0:T(8,128)S(1)} %get-tuple-element.103), channel_id=1, source_target_pairs={{2,0},{4,2},{6,4},{8,6},{10,8},{12,10},{14,12},{0,14},{3,1},{5,3},... | collective-permute-start | bytes 122888 | tf_op jit(solution)/shard_map/while/body/eval_jaxpr/ppermute | solution.py:30
  144.1 2.0 %collective-permute-done = f32[1,2,40,1,128]{4,2,3,1,0:T(8,128)S(1)} collective-permute-done((f32[1,2,40,1,128]{4,2,3,1,0:T(8,128)S(1)}, f32[1,2,40,1,128]{4,2,3,1,0:T(8,128)S(1)}, u32[]{:S(2)}, u32[]{:S(2)}) %collective-permute-start) | collective-permute-done | bytes 40992 | tf_op jit(solution)/shard_map/while/body/eval_jaxpr/ppermute | solution.py:28
  151.7 4.7 %collective-permute-start.1 = (f32[1,2,40,1,128]{4,2,3,1,0:T(8,128)S(1)}, f32[1,2,40,1,128]{4,2,3,1,0:T(8,128)S(1)}, u32[]{:S(2)}, u32[]{:S(2)}) collective-permute-start(f32[1,2,40,1,128]{4,2,3,1,0:T(8,128)S(1)} %get-tuple-element.103), channel_id=1, source_target_pairs={{2,0},{4,2},{6,4},{8,6},{10,8},{12,10},{14,12},{0,14},{3,1},{5,3},... | collective-permute-start | bytes 122888 | tf_op jit(solution)/shard_map/while/body/eval_jaxpr/ppermute | solution.py:30
  156.4 2.0 %collective-permute-done = f32[1,2,40,1,128]{4,2,3,1,0:T(8,128)S(1)} collective-permute-done((f32[1,2,40,1,128]{4,2,3,1,0:T(8,128)S(1)}, f32[1,2,40,1,128]{4,2,3,1,0:T(8,128)S(1)}, u32[]{:S(2)}, u32[]{:S(2)}) %collective-permute-start) | collective-permute-done | bytes 40992 | tf_op jit(solution)/shard_map/while/body/eval_jaxpr/ppermute | solution.py:28
  162.9 2.0 %copy.20 = f32[1,2,40,16,128]{4,3,2,1,0:T(8,128)} copy(f32[1,2,40,16,128]{4,2,3,1,0:T(8,128)} %get-tuple-element.32) | data formatting | bytes 1310720 | tf_op jit(solution)/shard_map/while | solution.py:81
  (196 shorter events, 54.5 us)
Async XLA Ops:
  6.5 30.4 %all-gather.2.cloned.1.call-start = ((), (), s32[]{:S(2)}) async-start(), calls=%async_computation | async-start | bytes 1966080 | tf_op jit(solution)/shard_map/all_gather | solution.py:59
  9.9 7.6 %collective-permute-start.4 = (f32[1,128]{1,0:T(1,128)S(1)}, f32[1,128]{1,0:T(1,128)S(1)}, u32[]{:S(2)}, u32[]{:S(2)}) collective-permute-start(f32[1,128]{1,0:T(1,128)S(1)} %slice_bitcast_fusion.1), channel_id=1, source_target_pairs={{14,0},{0,2},{2,4},{4,6},{6,8},{8,10},{10,12},{12,14},{15,1},{1,3}... | collective-permute-start | bytes 1544 | tf_op jit(solution)/shard_map/ppermute | solution.py:12
  13.0 2.3 %collective-permute-start.5 = (f32[16,1]{1,0:T(8,128)S(1)}, f32[16,1]{1,0:T(8,128)S(1)}, u32[]{:S(2)}, u32[]{:S(2)}) collective-permute-start(f32[16,1]{1,0:T(8,128)S(1)} %slice.63), channel_id=1, source_target_pairs={{0,1},{2,3},{4,5},{6,7},{8,9},{10,11},{12,13},{14,15},{16,17},{18,... | collective-permute-start | bytes 200 | tf_op jit(solution)/shard_map/ppermute | solution.py:18
  41.1 6.7 %collective-permute-start = (f32[1,2,40,1,128]{4,2,3,1,0:T(8,128)S(1)}, f32[1,2,40,1,128]{4,2,3,1,0:T(8,128)S(1)}, u32[]{:S(2)}, u32[]{:S(2)}) collective-permute-start(f32[1,2,40,1,128]{4,2,3,1,0:T(8,128)S(1)} %get-tuple-element.102), channel_id=1, source_target_pairs={{0,2},{2,4},{4,6},{6,8},{8,10},{10,12},{12,14},{14,0},{1,3},{3,5},... | collective-permute-start | bytes 122888 | tf_op jit(solution)/shard_map/while/body/eval_jaxpr/ppermute | solution.py:28
  42.6 5.2 %collective-permute-start.1 = (f32[1,2,40,1,128]{4,2,3,1,0:T(8,128)S(1)}, f32[1,2,40,1,128]{4,2,3,1,0:T(8,128)S(1)}, u32[]{:S(2)}, u32[]{:S(2)}) collective-permute-start(f32[1,2,40,1,128]{4,2,3,1,0:T(8,128)S(1)} %get-tuple-element.103), channel_id=1, source_target_pairs={{2,0},{4,2},{6,4},{8,6},{10,8},{12,10},{14,12},{0,14},{3,1},{5,3},... | collective-permute-start | bytes 122888 | tf_op jit(solution)/shard_map/while/body/eval_jaxpr/ppermute | solution.py:30
  48.7 1.8 %collective-permute-start.3 = (f32[1,2,40,18,1]{2,1,4,3,0:T(2,128)S(1)}, f32[1,2,40,18,1]{2,1,4,3,0:T(2,128)S(1)}, u32[]{:S(2)}, u32[]{:S(2)}) collective-permute-start(f32[1,2,40,18,1]{2,1,4,3,0:T(2,128)S(1)} %copy.34), channel_id=1, source_target_pairs={{1,0},{0,1},{3,2},{2,3},{5,4},{4,5},{7,6},{6,7},{9,8},{8,9},{11,10... | collective-permute-start | bytes 17288 | tf_op jit(solution)/shard_map/while/body/eval_jaxpr/ppermute | solution.py:30
  53.3 6.7 %collective-permute-start = (f32[1,2,40,1,128]{4,2,3,1,0:T(8,128)S(1)}, f32[1,2,40,1,128]{4,2,3,1,0:T(8,128)S(1)}, u32[]{:S(2)}, u32[]{:S(2)}) collective-permute-start(f32[1,2,40,1,128]{4,2,3,1,0:T(8,128)S(1)} %get-tuple-element.102), channel_id=1, source_target_pairs={{0,2},{2,4},{4,6},{6,8},{8,10},{10,12},{12,14},{14,0},{1,3},{3,5},... | collective-permute-start | bytes 122888 | tf_op jit(solution)/shard_map/while/body/eval_jaxpr/ppermute | solution.py:28
  54.5 5.7 %collective-permute-start.1 = (f32[1,2,40,1,128]{4,2,3,1,0:T(8,128)S(1)}, f32[1,2,40,1,128]{4,2,3,1,0:T(8,128)S(1)}, u32[]{:S(2)}, u32[]{:S(2)}) collective-permute-start(f32[1,2,40,1,128]{4,2,3,1,0:T(8,128)S(1)} %get-tuple-element.103), channel_id=1, source_target_pairs={{2,0},{4,2},{6,4},{8,6},{10,8},{12,10},{14,12},{0,14},{3,1},{5,3},... | collective-permute-start | bytes 122888 | tf_op jit(solution)/shard_map/while/body/eval_jaxpr/ppermute | solution.py:30
  61.0 1.8 %collective-permute-start.3 = (f32[1,2,40,18,1]{2,1,4,3,0:T(2,128)S(1)}, f32[1,2,40,18,1]{2,1,4,3,0:T(2,128)S(1)}, u32[]{:S(2)}, u32[]{:S(2)}) collective-permute-start(f32[1,2,40,18,1]{2,1,4,3,0:T(2,128)S(1)} %copy.34), channel_id=1, source_target_pairs={{1,0},{0,1},{3,2},{2,3},{5,4},{4,5},{7,6},{6,7},{9,8},{8,9},{11,10... | collective-permute-start | bytes 17288 | tf_op jit(solution)/shard_map/while/body/eval_jaxpr/ppermute | solution.py:30
  65.6 6.7 %collective-permute-start = (f32[1,2,40,1,128]{4,2,3,1,0:T(8,128)S(1)}, f32[1,2,40,1,128]{4,2,3,1,0:T(8,128)S(1)}, u32[]{:S(2)}, u32[]{:S(2)}) collective-permute-start(f32[1,2,40,1,128]{4,2,3,1,0:T(8,128)S(1)} %get-tuple-element.102), channel_id=1, source_target_pairs={{0,2},{2,4},{4,6},{6,8},{8,10},{10,12},{12,14},{14,0},{1,3},{3,5},... | collective-permute-start | bytes 122888 | tf_op jit(solution)/shard_map/while/body/eval_jaxpr/ppermute | solution.py:28
  65.7 6.7 %collective-permute-start.1 = (f32[1,2,40,1,128]{4,2,3,1,0:T(8,128)S(1)}, f32[1,2,40,1,128]{4,2,3,1,0:T(8,128)S(1)}, u32[]{:S(2)}, u32[]{:S(2)}) collective-permute-start(f32[1,2,40,1,128]{4,2,3,1,0:T(8,128)S(1)} %get-tuple-element.103), channel_id=1, source_target_pairs={{2,0},{4,2},{6,4},{8,6},{10,8},{12,10},{14,12},{0,14},{3,1},{5,3},... | collective-permute-start | bytes 122888 | tf_op jit(solution)/shard_map/while/body/eval_jaxpr/ppermute | solution.py:30
  73.3 1.8 %collective-permute-start.3 = (f32[1,2,40,18,1]{2,1,4,3,0:T(2,128)S(1)}, f32[1,2,40,18,1]{2,1,4,3,0:T(2,128)S(1)}, u32[]{:S(2)}, u32[]{:S(2)}) collective-permute-start(f32[1,2,40,18,1]{2,1,4,3,0:T(2,128)S(1)} %copy.34), channel_id=1, source_target_pairs={{1,0},{0,1},{3,2},{2,3},{5,4},{4,5},{7,6},{6,7},{9,8},{8,9},{11,10... | collective-permute-start | bytes 17288 | tf_op jit(solution)/shard_map/while/body/eval_jaxpr/ppermute | solution.py:30
  77.9 6.7 %collective-permute-start = (f32[1,2,40,1,128]{4,2,3,1,0:T(8,128)S(1)}, f32[1,2,40,1,128]{4,2,3,1,0:T(8,128)S(1)}, u32[]{:S(2)}, u32[]{:S(2)}) collective-permute-start(f32[1,2,40,1,128]{4,2,3,1,0:T(8,128)S(1)} %get-tuple-element.102), channel_id=1, source_target_pairs={{0,2},{2,4},{4,6},{6,8},{8,10},{10,12},{12,14},{14,0},{1,3},{3,5},... | collective-permute-start | bytes 122888 | tf_op jit(solution)/shard_map/while/body/eval_jaxpr/ppermute | solution.py:28
  77.9 6.8 %collective-permute-start.1 = (f32[1,2,40,1,128]{4,2,3,1,0:T(8,128)S(1)}, f32[1,2,40,1,128]{4,2,3,1,0:T(8,128)S(1)}, u32[]{:S(2)}, u32[]{:S(2)}) collective-permute-start(f32[1,2,40,1,128]{4,2,3,1,0:T(8,128)S(1)} %get-tuple-element.103), channel_id=1, source_target_pairs={{2,0},{4,2},{6,4},{8,6},{10,8},{12,10},{14,12},{0,14},{3,1},{5,3},... | collective-permute-start | bytes 122888 | tf_op jit(solution)/shard_map/while/body/eval_jaxpr/ppermute | solution.py:30
  85.6 1.8 %collective-permute-start.3 = (f32[1,2,40,18,1]{2,1,4,3,0:T(2,128)S(1)}, f32[1,2,40,18,1]{2,1,4,3,0:T(2,128)S(1)}, u32[]{:S(2)}, u32[]{:S(2)}) collective-permute-start(f32[1,2,40,18,1]{2,1,4,3,0:T(2,128)S(1)} %copy.34), channel_id=1, source_target_pairs={{1,0},{0,1},{3,2},{2,3},{5,4},{4,5},{7,6},{6,7},{9,8},{8,9},{11,10... | collective-permute-start | bytes 17288 | tf_op jit(solution)/shard_map/while/body/eval_jaxpr/ppermute | solution.py:30
  90.2 6.7 %collective-permute-start = (f32[1,2,40,1,128]{4,2,3,1,0:T(8,128)S(1)}, f32[1,2,40,1,128]{4,2,3,1,0:T(8,128)S(1)}, u32[]{:S(2)}, u32[]{:S(2)}) collective-permute-start(f32[1,2,40,1,128]{4,2,3,1,0:T(8,128)S(1)} %get-tuple-element.102), channel_id=1, source_target_pairs={{0,2},{2,4},{4,6},{6,8},{8,10},{10,12},{12,14},{14,0},{1,3},{3,5},... | collective-permute-start | bytes 122888 | tf_op jit(solution)/shard_map/while/body/eval_jaxpr/ppermute | solution.py:28
  90.2 6.7 %collective-permute-start.1 = (f32[1,2,40,1,128]{4,2,3,1,0:T(8,128)S(1)}, f32[1,2,40,1,128]{4,2,3,1,0:T(8,128)S(1)}, u32[]{:S(2)}, u32[]{:S(2)}) collective-permute-start(f32[1,2,40,1,128]{4,2,3,1,0:T(8,128)S(1)} %get-tuple-element.103), channel_id=1, source_target_pairs={{2,0},{4,2},{6,4},{8,6},{10,8},{12,10},{14,12},{0,14},{3,1},{5,3},... | collective-permute-start | bytes 122888 | tf_op jit(solution)/shard_map/while/body/eval_jaxpr/ppermute | solution.py:30
  97.9 1.8 %collective-permute-start.3 = (f32[1,2,40,18,1]{2,1,4,3,0:T(2,128)S(1)}, f32[1,2,40,18,1]{2,1,4,3,0:T(2,128)S(1)}, u32[]{:S(2)}, u32[]{:S(2)}) collective-permute-start(f32[1,2,40,18,1]{2,1,4,3,0:T(2,128)S(1)} %copy.34), channel_id=1, source_target_pairs={{1,0},{0,1},{3,2},{2,3},{5,4},{4,5},{7,6},{6,7},{9,8},{8,9},{11,10... | collective-permute-start | bytes 17288 | tf_op jit(solution)/shard_map/while/body/eval_jaxpr/ppermute | solution.py:30
  102.5 6.7 %collective-permute-start = (f32[1,2,40,1,128]{4,2,3,1,0:T(8,128)S(1)}, f32[1,2,40,1,128]{4,2,3,1,0:T(8,128)S(1)}, u32[]{:S(2)}, u32[]{:S(2)}) collective-permute-start(f32[1,2,40,1,128]{4,2,3,1,0:T(8,128)S(1)} %get-tuple-element.102), channel_id=1, source_target_pairs={{0,2},{2,4},{4,6},{6,8},{8,10},{10,12},{12,14},{14,0},{1,3},{3,5},... | collective-permute-start | bytes 122888 | tf_op jit(solution)/shard_map/while/body/eval_jaxpr/ppermute | solution.py:28
  102.5 6.8 %collective-permute-start.1 = (f32[1,2,40,1,128]{4,2,3,1,0:T(8,128)S(1)}, f32[1,2,40,1,128]{4,2,3,1,0:T(8,128)S(1)}, u32[]{:S(2)}, u32[]{:S(2)}) collective-permute-start(f32[1,2,40,1,128]{4,2,3,1,0:T(8,128)S(1)} %get-tuple-element.103), channel_id=1, source_target_pairs={{2,0},{4,2},{6,4},{8,6},{10,8},{12,10},{14,12},{0,14},{3,1},{5,3},... | collective-permute-start | bytes 122888 | tf_op jit(solution)/shard_map/while/body/eval_jaxpr/ppermute | solution.py:30
  110.2 1.8 %collective-permute-start.3 = (f32[1,2,40,18,1]{2,1,4,3,0:T(2,128)S(1)}, f32[1,2,40,18,1]{2,1,4,3,0:T(2,128)S(1)}, u32[]{:S(2)}, u32[]{:S(2)}) collective-permute-start(f32[1,2,40,18,1]{2,1,4,3,0:T(2,128)S(1)} %copy.34), channel_id=1, source_target_pairs={{1,0},{0,1},{3,2},{2,3},{5,4},{4,5},{7,6},{6,7},{9,8},{8,9},{11,10... | collective-permute-start | bytes 17288 | tf_op jit(solution)/shard_map/while/body/eval_jaxpr/ppermute | solution.py:30
  114.8 6.7 %collective-permute-start = (f32[1,2,40,1,128]{4,2,3,1,0:T(8,128)S(1)}, f32[1,2,40,1,128]{4,2,3,1,0:T(8,128)S(1)}, u32[]{:S(2)}, u32[]{:S(2)}) collective-permute-start(f32[1,2,40,1,128]{4,2,3,1,0:T(8,128)S(1)} %get-tuple-element.102), channel_id=1, source_target_pairs={{0,2},{2,4},{4,6},{6,8},{8,10},{10,12},{12,14},{14,0},{1,3},{3,5},... | collective-permute-start | bytes 122888 | tf_op jit(solution)/shard_map/while/body/eval_jaxpr/ppermute | solution.py:28
  114.8 6.7 %collective-permute-start.1 = (f32[1,2,40,1,128]{4,2,3,1,0:T(8,128)S(1)}, f32[1,2,40,1,128]{4,2,3,1,0:T(8,128)S(1)}, u32[]{:S(2)}, u32[]{:S(2)}) collective-permute-start(f32[1,2,40,1,128]{4,2,3,1,0:T(8,128)S(1)} %get-tuple-element.103), channel_id=1, source_target_pairs={{2,0},{4,2},{6,4},{8,6},{10,8},{12,10},{14,12},{0,14},{3,1},{5,3},... | collective-permute-start | bytes 122888 | tf_op jit(solution)/shard_map/while/body/eval_jaxpr/ppermute | solution.py:30
  122.5 1.8 %collective-permute-start.3 = (f32[1,2,40,18,1]{2,1,4,3,0:T(2,128)S(1)}, f32[1,2,40,18,1]{2,1,4,3,0:T(2,128)S(1)}, u32[]{:S(2)}, u32[]{:S(2)}) collective-permute-start(f32[1,2,40,18,1]{2,1,4,3,0:T(2,128)S(1)} %copy.34), channel_id=1, source_target_pairs={{1,0},{0,1},{3,2},{2,3},{5,4},{4,5},{7,6},{6,7},{9,8},{8,9},{11,10... | collective-permute-start | bytes 17288 | tf_op jit(solution)/shard_map/while/body/eval_jaxpr/ppermute | solution.py:30
  127.1 6.7 %collective-permute-start = (f32[1,2,40,1,128]{4,2,3,1,0:T(8,128)S(1)}, f32[1,2,40,1,128]{4,2,3,1,0:T(8,128)S(1)}, u32[]{:S(2)}, u32[]{:S(2)}) collective-permute-start(f32[1,2,40,1,128]{4,2,3,1,0:T(8,128)S(1)} %get-tuple-element.102), channel_id=1, source_target_pairs={{0,2},{2,4},{4,6},{6,8},{8,10},{10,12},{12,14},{14,0},{1,3},{3,5},... | collective-permute-start | bytes 122888 | tf_op jit(solution)/shard_map/while/body/eval_jaxpr/ppermute | solution.py:28
  127.1 6.8 %collective-permute-start.1 = (f32[1,2,40,1,128]{4,2,3,1,0:T(8,128)S(1)}, f32[1,2,40,1,128]{4,2,3,1,0:T(8,128)S(1)}, u32[]{:S(2)}, u32[]{:S(2)}) collective-permute-start(f32[1,2,40,1,128]{4,2,3,1,0:T(8,128)S(1)} %get-tuple-element.103), channel_id=1, source_target_pairs={{2,0},{4,2},{6,4},{8,6},{10,8},{12,10},{14,12},{0,14},{3,1},{5,3},... | collective-permute-start | bytes 122888 | tf_op jit(solution)/shard_map/while/body/eval_jaxpr/ppermute | solution.py:30
  134.8 1.8 %collective-permute-start.3 = (f32[1,2,40,18,1]{2,1,4,3,0:T(2,128)S(1)}, f32[1,2,40,18,1]{2,1,4,3,0:T(2,128)S(1)}, u32[]{:S(2)}, u32[]{:S(2)}) collective-permute-start(f32[1,2,40,18,1]{2,1,4,3,0:T(2,128)S(1)} %copy.34), channel_id=1, source_target_pairs={{1,0},{0,1},{3,2},{2,3},{5,4},{4,5},{7,6},{6,7},{9,8},{8,9},{11,10... | collective-permute-start | bytes 17288 | tf_op jit(solution)/shard_map/while/body/eval_jaxpr/ppermute | solution.py:30
  139.4 6.7 %collective-permute-start = (f32[1,2,40,1,128]{4,2,3,1,0:T(8,128)S(1)}, f32[1,2,40,1,128]{4,2,3,1,0:T(8,128)S(1)}, u32[]{:S(2)}, u32[]{:S(2)}) collective-permute-start(f32[1,2,40,1,128]{4,2,3,1,0:T(8,128)S(1)} %get-tuple-element.102), channel_id=1, source_target_pairs={{0,2},{2,4},{4,6},{6,8},{8,10},{10,12},{12,14},{14,0},{1,3},{3,5},... | collective-permute-start | bytes 122888 | tf_op jit(solution)/shard_map/while/body/eval_jaxpr/ppermute | solution.py:28
  139.4 6.7 %collective-permute-start.1 = (f32[1,2,40,1,128]{4,2,3,1,0:T(8,128)S(1)}, f32[1,2,40,1,128]{4,2,3,1,0:T(8,128)S(1)}, u32[]{:S(2)}, u32[]{:S(2)}) collective-permute-start(f32[1,2,40,1,128]{4,2,3,1,0:T(8,128)S(1)} %get-tuple-element.103), channel_id=1, source_target_pairs={{2,0},{4,2},{6,4},{8,6},{10,8},{12,10},{14,12},{0,14},{3,1},{5,3},... | collective-permute-start | bytes 122888 | tf_op jit(solution)/shard_map/while/body/eval_jaxpr/ppermute | solution.py:30
  147.0 1.8 %collective-permute-start.3 = (f32[1,2,40,18,1]{2,1,4,3,0:T(2,128)S(1)}, f32[1,2,40,18,1]{2,1,4,3,0:T(2,128)S(1)}, u32[]{:S(2)}, u32[]{:S(2)}) collective-permute-start(f32[1,2,40,18,1]{2,1,4,3,0:T(2,128)S(1)} %copy.34), channel_id=1, source_target_pairs={{1,0},{0,1},{3,2},{2,3},{5,4},{4,5},{7,6},{6,7},{9,8},{8,9},{11,10... | collective-permute-start | bytes 17288 | tf_op jit(solution)/shard_map/while/body/eval_jaxpr/ppermute | solution.py:30
  151.7 6.7 %collective-permute-start = (f32[1,2,40,1,128]{4,2,3,1,0:T(8,128)S(1)}, f32[1,2,40,1,128]{4,2,3,1,0:T(8,128)S(1)}, u32[]{:S(2)}, u32[]{:S(2)}) collective-permute-start(f32[1,2,40,1,128]{4,2,3,1,0:T(8,128)S(1)} %get-tuple-element.102), channel_id=1, source_target_pairs={{0,2},{2,4},{4,6},{6,8},{8,10},{10,12},{12,14},{14,0},{1,3},{3,5},... | collective-permute-start | bytes 122888 | tf_op jit(solution)/shard_map/while/body/eval_jaxpr/ppermute | solution.py:28
  151.7 6.8 %collective-permute-start.1 = (f32[1,2,40,1,128]{4,2,3,1,0:T(8,128)S(1)}, f32[1,2,40,1,128]{4,2,3,1,0:T(8,128)S(1)}, u32[]{:S(2)}, u32[]{:S(2)}) collective-permute-start(f32[1,2,40,1,128]{4,2,3,1,0:T(8,128)S(1)} %get-tuple-element.103), channel_id=1, source_target_pairs={{2,0},{4,2},{6,4},{8,6},{10,8},{12,10},{14,12},{0,14},{3,1},{5,3},... | collective-permute-start | bytes 122888 | tf_op jit(solution)/shard_map/while/body/eval_jaxpr/ppermute | solution.py:30
  (13 other events, 47.7 us)
Sparse Core Ops, SparseCore 0:
  10.0 26.9 all-gather.1
where the time goes:
time: 172 us
  starting transfers between devices  57.3 us (33%)
  waiting for transfers between devices  49.7 us (29%)
  local copies, waits for them, and re-layouts  29.9 us (17%)
  other arithmetic  17.9 us (10%)
  between operations  13.4 us (8%)
  matrix products  3.01 us (2%)
    ppermute x20, starting transfers between devices, padded(): lax.ppermute(head, axis, [((i + 1) % count, i) for i in range(count)])  45.2 us
    ppermute x20, waiting for transfers between devices, padded(): lax.ppermute(tail, axis, [(i, (i + 1) % count) for i in range(count)])  27.5 us
    all_gather x1, waiting for transfers between devices, per_device(): lax.all_gather(masked, 'lev', axis=2, tiled=True)  19.4 us
    while x50, local copies, waits for them, and re-layouts  17.4 us
    mul x10, other arithmetic, relax(): return wet_center * (center + flux)  14.5 us
    ppermute x20, starting transfers between devices, padded(): lax.ppermute(tail, axis, [(i, (i + 1) % count) for i in range(count)])  7.65 us
  transfers between devices with their start and end apart: 43, of which 23 were waited for; matrix products, arithmetic and copies ran while one was open for 3% of the time, Pallas kernels for 0%

commit v1 on v0

--- a/solution.py
+++ b/solution.py
@@ -1,6 +1,8 @@
 import jax
 import jax.numpy as jnp
 from jax import lax
+from jax.experimental import pallas as pl
+from jax.experimental.pallas import tpu as pltpu
 from jax.sharding import PartitionSpec as P
 
 PASSES = 10
@@ -82,6 +84,240 @@
     return field
 
 
+TILE = 8
+LANES = 128
+WIDTH = 5
+PARTS = 4
+MESH = pl.DeviceIdType.MESH
+
+
+def remote(src, dst, send_sem, recv_sem, device):
+    return pltpu.make_async_remote_copy(
+        src_ref=src,
+        dst_ref=dst,
+        send_sem=send_sem,
+        recv_sem=recv_sem,
+        device_id=device,
+        device_id_type=MESH,
+    )
+
+
+def kernel(
+    masked_ref, geo_ref, corr_ref, out_ref,
+    geo, own, other, field, halo, east, north,
+    own_sems, same_sems, cross_sems, geo_sems, halo_sems, out_sems,
+):
+    lev, gx, gy = lax.axis_index("lev"), lax.axis_index("gx"), lax.axis_index("gy")
+    count = lax.axis_size("gx")
+    cells = masked_ref.shape[1]
+    levels = masked_ref.shape[2]
+    tiles = levels // TILE
+    width = WIDTH
+    rows = cells + 2 * width
+    rounds = PASSES // width
+    east_dev = {"gx": lax.rem(gx + 1, count)}
+    west_dev = {"gx": lax.rem(gx + count - 1, count)}
+    mate = {"gy": 1 - gy}
+    pair = {"lev": 1 - lev}
+    cross = {"lev": 1 - lev, "gy": 1 - gy}
+
+    barrier = pltpu.get_barrier_semaphore()
+    everyone = (east_dev, west_dev, mate, pair, cross)
+    for device in everyone:
+        pl.semaphore_signal(barrier, inc=1, device_id=device, device_id_type=MESH)
+    pl.semaphore_wait(barrier, len(everyone))
+
+    part = cells // PARTS
+    spans = [pl.ds(q * part, part) for q in range(PARTS)]
+    own_copies, same_copies, cross_copies = [], [], []
+    order = [0, PARTS - 1] + list(range(1, PARTS - 1))
+    for q in order:
+        same_copies.append(remote(
+            masked_ref.at[gy, spans[q]], other.at[gy, spans[q]],
+            same_sems.at[0, q], same_sems.at[1, q], pair))
+        cross_copies.append(remote(
+            masked_ref.at[1 - gy, spans[q]], other.at[gy, spans[q]],
+            cross_sems.at[0, q], cross_sems.at[1, q], cross))
+        same_copies[-1].start()
+        cross_copies[-1].start()
+    geo_copies = [
+        remote(geo_ref, geo.at[gy, pl.ds(width, cells)], geo_sems.at[0, 0], geo_sems.at[1, 0], mate),
+        remote(geo_ref.at[pl.ds(cells - width, width)], geo.at[gy, pl.ds(0, width)],
+               geo_sems.at[0, 1], geo_sems.at[1, 1], east_dev),
+        remote(geo_ref.at[pl.ds(0, width)], geo.at[gy, pl.ds(width + cells, width)],
+               geo_sems.at[0, 2], geo_sems.at[1, 2], west_dev),
+    ]
+    for copy in geo_copies:
+        copy.start()
+    own_copy = remote(masked_ref.at[1 - gy], own, own_sems.at[0], own_sems.at[1], mate)
+    own_copy.start()
+
+    geo[gy, width:width + cells] = geo_ref[...]
+    corr = corr_ref[...]
+    high = corr.astype(jnp.bfloat16)
+    low = (corr - high.astype(jnp.float32)).astype(jnp.bfloat16)
+    weights = jnp.concatenate([high, high, low], axis=1)
+
+    own_copy.wait()
+    geo_copies[0].wait()
+    forward = []
+    for side, start in ((1, 0), (2, width + cells)):
+        geo_copies[side].wait()
+        forward.append(remote(
+            geo.at[gy, pl.ds(start, width)], geo.at[gy, pl.ds(start, width)],
+            geo_sems.at[0, 2 + side], geo_sems.at[1, 2 + side], mate))
+        forward[-1].start()
+
+    def send_halo(r, k):
+        copies = (
+            remote(field.at[k, pl.ds(width, width)], halo.at[r, 1, k],
+                   halo_sems.at[0, r, 0, k], halo_sems.at[1, r, 0, k], west_dev),
+            remote(field.at[k, pl.ds(cells, width)], halo.at[r, 0, k],
+                   halo_sems.at[0, r, 1, k], halo_sems.at[1, r, 1, k], east_dev),
+        )
+        for copy in copies:
+            copy.start()
+        return copies
+
+    def vertical(x):
+        mine = masked_ref[gy, x]
+        theirs = own[x]
+        first = jnp.where(gy == 0, mine, theirs)
+        second = jnp.where(gy == 0, theirs, mine)
+        near = jnp.concatenate([first, second], axis=1)
+        far = jnp.concatenate([other[0, x], other[1, x]], axis=1)
+        both = jnp.concatenate([near, far], axis=0)
+        top = both.astype(jnp.bfloat16)
+        rest = (both - top.astype(jnp.float32)).astype(jnp.bfloat16)
+        stack = jnp.concatenate([top, rest, top], axis=0)
+        result = jnp.dot(weights, stack, preferred_element_type=jnp.float32)
+        for half in range(2):
+            for k in range(tiles):
+                value = result[k * TILE:(k + 1) * TILE, half * LANES:(half + 1) * LANES]
+                wet = geo[half, width + x, k * TILE:(k + 1) * TILE]
+                field[k, width + x, half] = value * wet
+
+    for place, q in enumerate(order):
+        same_copies[place].wait()
+        cross_copies[place].wait()
+        for x in range(q * part, (q + 1) * part):
+            vertical(x)
+
+    pending = [send_halo(0, k) for k in range(tiles)]
+
+    for copy in forward:
+        copy.wait()
+    for half in range(2):
+        for row in range(rows):
+            east[row, half] = jnp.broadcast_to(geo[half, row, levels:levels + 1], (TILE, LANES))
+            north[row, half] = jnp.broadcast_to(geo[half, row, levels + 1:levels + 2], (TILE, LANES))
+
+    lane = lax.broadcasted_iota(jnp.int32, (TILE, LANES), 1)
+    at_end = lane == LANES - 1
+    at_start = lane == 0
+
+    def relax_tile(r, k):
+        for step in range(width):
+            def row_of(row):
+                if step == 0 and row < width:
+                    return halo[r, 0, k, row, 0], halo[r, 0, k, row, 1]
+                if step == 0 and row >= width + cells:
+                    at = row - width - cells
+                    return halo[r, 1, k, at, 0], halo[r, 1, k, at, 1]
+                return field[k, row, 0], field[k, row, 1]
+
+            first, last = step + 1, rows - 2 - step
+            before, here = row_of(first - 1), row_of(first)
+            flux = [east[first - 1, h] * (here[h] - before[h]) for h in range(2)]
+            for row in range(first, last + 1):
+                after = row_of(row + 1)
+                turned = [pltpu.roll(here[h], LANES - 1, 1) for h in range(2)]
+                up = [jnp.where(at_end, turned[1], turned[0]), turned[1]]
+                rise = [north[row, h] * (up[h] - here[h]) for h in range(2)]
+                back = [pltpu.roll(rise[h], 1, 1) for h in range(2)]
+                down = [jnp.where(at_start, back[1], back[0]), jnp.where(at_start, back[0], back[1])]
+                ahead = [east[row, h] * (after[h] - here[h]) for h in range(2)]
+                for h in range(2):
+                    wet = geo[h, row, k * TILE:(k + 1) * TILE]
+                    total = here[h] + ((ahead[h] - flux[h]) + (rise[h] - down[h]))
+                    field[k, row, h] = wet * total
+                here, flux = after, ahead
+
+    out_copies = []
+    for r in range(rounds):
+        later = []
+        for k in range(tiles):
+            for copy in pending[k]:
+                copy.wait()
+            relax_tile(r, k)
+            if r < rounds - 1:
+                later.append(send_halo(r + 1, k))
+            else:
+                out_copies.append(remote(
+                    field.at[k, pl.ds(width, cells), 1 - gy], out_ref.at[gy, k],
+                    out_sems.at[0, k], out_sems.at[1, k], mate))
+                out_copies[-1].start()
+                out_ref[gy, k] = field[k, width:width + cells, gy]
+        pending = later
+    for copy in out_copies:
+        copy.wait()
+
+
+def fused(increments, vert_corr, kappa, sea_mask, level_count):
+    levels, cells, lanes = sea_mask.shape
+    tiles = levels // TILE
+    width = WIDTH
+    rows = cells + 2 * width
+    rounds = PASSES // width
+    gy = lax.axis_index("gy")
+    lev = lax.axis_index("lev")
+    numbers = lev * levels + jnp.arange(levels, dtype=jnp.int32)
+    turned = jnp.swapaxes(sea_mask, 0, 1)
+    wet = (turned * (numbers[None, :, None] < level_count[:, None, :]).astype(jnp.int32)).astype(jnp.float32)
+    masked = jnp.swapaxes(increments[0], 1, 2) * wet[None]
+    total_y = lanes * lax.axis_size("gy")
+    local_rows = gy * lanes + jnp.arange(lanes, dtype=jnp.int32)
+    north = kappa[1] * (local_rows != total_y - 1).astype(jnp.float32)[None]
+    fill = jnp.zeros((cells, TILE - 2, lanes), jnp.float32)
+    geo = jnp.concatenate([wet, kappa[0][:, None], north[:, None], fill], axis=1)
+    mine = lax.dynamic_slice(vert_corr, (gy, lev * levels, 0), (1, levels, 2 * levels))[0]
+    corr = jnp.where(lev == 0, mine, jnp.roll(mine, levels, 1))
+    vmem = pl.BlockSpec(memory_space=pltpu.VMEM)
+    f32 = jnp.float32
+    dma = pltpu.SemaphoreType.DMA
+    result = pl.pallas_call(
+        kernel,
+        out_shape=jax.ShapeDtypeStruct((2, tiles, cells, TILE, lanes), f32),
+        in_specs=[vmem] * 3,
+        out_specs=vmem,
+        scratch_shapes=[
+            pltpu.VMEM((2, rows, levels + TILE, lanes), f32),
+            pltpu.VMEM((cells, levels, lanes), f32),
+            pltpu.VMEM((2, cells, levels, lanes), f32),
+            pltpu.VMEM((tiles, rows, 2, TILE, lanes), f32),
+            pltpu.VMEM((rounds, 2, tiles, width, 2, TILE, lanes), f32),
+            pltpu.VMEM((rows, 2, TILE, lanes), f32),
+            pltpu.VMEM((rows, 2, TILE, lanes), f32),
+            dma((2,)),
+            dma((2, PARTS)),
+            dma((2, PARTS)),
+            dma((2, 5)),
+            dma((2, rounds, 2, tiles)),
+            dma((2, tiles)),
+        ],
+        compiler_params=pltpu.CompilerParams(
+            collective_id=0, has_side_effects=True, vmem_limit_bytes=32 * 1024 * 1024
+        ),
+        cost_estimate=pl.CostEstimate(flops=60_000_000, bytes_accessed=4_000_000, transcendentals=0),
+    )(masked, geo, corr)
+    return result.transpose(0, 1, 3, 2, 4).reshape(increments.shape)
+
+
+def fits(mesh):
+    shape = mesh.shape
+    return shape["lev"] == 2 and shape["gy"] == 2 and shape["gx"] > 2
+
+
 def solution(mesh):
     in_specs = (
         P(None, None, "lev", "gx", "gy"),
@@ -92,5 +328,5 @@
     )
     out_specs = P(None, None, "lev", "gx", "gy")
     return jax.shard_map(
-        per_device, mesh=mesh, in_specs=in_specs, out_specs=out_specs, check_vma=False
-    )
+        fused if fits(mesh) else per_device, mesh=mesh, in_specs=in_specs, out_specs=out_specs, check_vma=False
+    )

time: 172 us -> 47.7 us (0.28)
  starting transfers between devices: 57.3 us -> 0 us
  waiting for transfers between devices: 49.7 us -> 0 us
  Pallas kernels: 0 us -> 43.3 us
  local copies, waits for them, and re-layouts: 29.9 us -> 2.51 us
  other arithmetic: 17.9 us -> 1.56 us
  between operations: 13.4 us -> 0.05 us
  matrix products: 3.01 us -> 0 us
    ppermute x42 -> x0, starting transfers between devices: 57.3 us -> none  [the longest x20 45.2 us: padded(): lax.ppermute(head, axis, [((i + 1) % count, i) for i in range(count)])]
    pallas_call x0 -> x1, Pallas kernels: none -> 43.3 us  [fused(): pl.pallas_call(kernel, out_shape=jax.ShapeDtypeStruct((2, tiles, cells, T...]
    ppermute x42 -> x0, waiting for transfers between devices: 30.4 us -> none  [the longest x20 27.5 us: padded(): lax.ppermute(tail, axis, [(i, (i + 1) % count) for i in range(count)])]
    while x51 -> x0, local copies, waits for them, and re-layouts: 19.5 us -> none
    all_gather x1 -> x0, waiting for transfers between devices: 19.4 us -> none  [per_device(): lax.all_gather(masked, 'lev', axis=2, tiled=True)]
    mul x12 -> x2, other arithmetic: 16.7 us -> 0.22 us  [the longest x1 0.21 us: fused(): masked = jnp.swapaxes(increments[0], 1, 2) * wet[None]]
    ppermute x20 -> x0, local copies, waits for them, and re-layouts: 6.61 us -> none  [the longest x10 3.31 us: padded(): lax.ppermute(head, axis, [((i + 1) % count, i) for i in range(count)])]
    dot_general x1 -> x0, matrix products: 3.01 us -> none  [per_device(): jnp.einsum('toh,dthxy->dtoxy', own_rows, lax.all_gather(masked, 'lev', ax...]
  transfers between devices with their start and end apart: 43 -> 0, of which waited for: 23 -> 0; matrix products, arithmetic and copies ran while one was open for 3% -> 0% of each run, Pallas kernels for 0% -> 0%
where the time goes in v1:
time: 47.7 us; the launch traced here: 47.5 us
  Pallas kernels  43.3 us (91%)
  local copies, waits for them, and re-layouts  2.51 us (5%)
  other arithmetic  1.56 us (3%)
    pallas_call x1, Pallas kernels, fused(): pl.pallas_call(kernel, out_shape=jax.ShapeDtypeStruct((2, tiles, cells, T...  43.3 us
    convert_element_type x1, other arithmetic, fused(): (turned * (numbers[None, :, None] < level_count[:, None, :]).astype(jnp.i...  1.15 us

profile of v1, /device:TPU:0, one launch (start us, length us, event | category | flops | bytes accessed | tf_op | source)
XLA Modules:
  0.0 47.5 jit_solution(1641399449318226120)
XLA Ops:
  0.0 0.0 copy-start.1
  0.0 0.1 pad.5.clone
  0.1 0.7 %fusion.2 = (f32[1,16,128]{2,1,0:T(8,128)S(1)}, f32[1,16,128]{2,1,0:T(8,128)S(1)}) fusion(f32[2,16,128]{2,1,0:T(8,128)} %param.7), kind=kLoop, calls=%fused_computation.10 | loop fusion | bytes 32768 | tf_op jit(solution)/shard_map/slice | solution.py:282
  0.8 0.1 copy-done.1
  0.9 0.1 fusion.1
  1.0 0.0 copy-start.2
  1.0 0.1 maximum_select_fusion.corr_ref
  1.0 0.6 %copy-done.2 = s32[16,128]{1,0:T(8,128)S(1)} copy-done((s32[16,128]{1,0:T(8,128)S(1)}, s32[16,128]{1,0:T(8,128)}, u32[]{:S(2)}) %copy-start.2) | copy-done | bytes 8216
  1.7 0.0 copy-start
  1.7 1.2 %fusion = f32[16,40,128]{2,1,0:T(8,128)S(1)} fusion(s32[40,16,128]{2,1,0:T(8,128)} %param.8, s32[16,128]{1,0:T(8,128)S(1)} %copy-done.2, s32[40]{0:T(128)S(1)} %iota_add_fusion), kind=kLoop, calls=%fused_computation.3 | loop fusion | flops 245760 | bytes 663712 | tf_op jit(solution)/shard_map/convert_element_type | solution.py:276
  2.8 0.1 maximum_maximum_fusion.geo_ref
  2.9 0.0 copy-done
  2.9 0.2 bitcast_multiply_fusion.masked_ref
  3.2 43.3 %shard_map.55 = f32[2,5,16,8,128]{4,3,2,1,0:T(8,128)S(1)} custom-call(f32[2,16,40,128]{3,2,1,0:T(8,128)S(1)} %bitcast_multiply_fusion.masked_ref, f32[16,48,128]{2,1,0:T(8,128)S(1)} %maximum_maximum_fusion.geo_ref, f32[40,80]{1,0:T(8,128)S(1)} %maximum_select_fusion.corr_ref), custom_call_target="tpu_custom_call" | custom-call | flops 60000000 | bytes 4000000 | tf_op jit(solution)/shard_map/pallas_call | solution.py:288
  46.5 1.0 %copy.10 = f32[2,5,8,16,128]{4,3,2,1,0:T(8,128)} copy(f32[2,5,8,16,128]{4,2,3,1,0:T(8,128)S(1)} %bitcast.16) | data formatting | bytes 1310720 | tf_op jit(solution)/shard_map/transpose | solution.py:313
  (5 shorter events, 0.0 us)
Async XLA Ops:
  0.0 0.9 %copy-start.1 = (f32[2,80,80]{2,1,0:T(8,128)S(1)}, f32[2,80,80]{2,1,0:T(8,128)}, u32[]{:S(2)}) copy-start(f32[2,80,80]{2,1,0:T(8,128)} %param.6) | copy-start | bytes 153604
  1.0 0.7 %copy-start.2 = (s32[16,128]{1,0:T(8,128)S(1)}, s32[16,128]{1,0:T(8,128)}, u32[]{:S(2)}) copy-start(s32[16,128]{1,0:T(8,128)} %param.9) | copy-start | bytes 24580
  1.7 1.3 %copy-start = (f32[1,2,40,16,128]{4,3,2,1,0:T(8,128)S(1)}, f32[1,2,40,16,128]{4,3,2,1,0:T(8,128)}, u32[]{:S(2)}) copy-start(f32[1,2,40,16,128]{4,3,2,1,0:T(8,128)} %param.5) | copy-start | bytes 1966084

commit v2 on v1

--- a/solution.py
+++ b/solution.py
@@ -87,7 +87,6 @@
 TILE = 8
 LANES = 128
 WIDTH = 5
-PARTS = 4
 MESH = pl.DeviceIdType.MESH
 
 
@@ -127,30 +126,35 @@
         pl.semaphore_signal(barrier, inc=1, device_id=device, device_id_type=MESH)
     pl.semaphore_wait(barrier, len(everyone))
 
-    part = cells // PARTS
-    spans = [pl.ds(q * part, part) for q in range(PARTS)]
+    starts = ((0, width), (cells - width, width), (width, cells - 2 * width))
     own_copies, same_copies, cross_copies = [], [], []
-    order = [0, PARTS - 1] + list(range(1, PARTS - 1))
-    for q in order:
+    for q, (start, size) in enumerate(starts):
+        span = pl.ds(start, size)
+        own_copies.append(remote(
+            masked_ref.at[1 - gy, span], own.at[span], own_sems.at[0, q], own_sems.at[1, q], mate))
         same_copies.append(remote(
-            masked_ref.at[gy, spans[q]], other.at[gy, spans[q]],
+            masked_ref.at[gy, span], other.at[gy, span],
             same_sems.at[0, q], same_sems.at[1, q], pair))
         cross_copies.append(remote(
-            masked_ref.at[1 - gy, spans[q]], other.at[gy, spans[q]],
+            masked_ref.at[1 - gy, span], other.at[gy, span],
             cross_sems.at[0, q], cross_sems.at[1, q], cross))
-        same_copies[-1].start()
-        cross_copies[-1].start()
     geo_copies = [
         remote(geo_ref, geo.at[gy, pl.ds(width, cells)], geo_sems.at[0, 0], geo_sems.at[1, 0], mate),
-        remote(geo_ref.at[pl.ds(cells - width, width)], geo.at[gy, pl.ds(0, width)],
+        remote(geo_ref.at[pl.ds(cells - width, width)],
+               geo.at[gy, pl.ds(0, width)],
                geo_sems.at[0, 1], geo_sems.at[1, 1], east_dev),
-        remote(geo_ref.at[pl.ds(0, width)], geo.at[gy, pl.ds(width + cells, width)],
+        remote(geo_ref.at[pl.ds(0, width)],
+               geo.at[gy, pl.ds(width + cells, width)],
                geo_sems.at[0, 2], geo_sems.at[1, 2], west_dev),
     ]
-    for copy in geo_copies:
-        copy.start()
-    own_copy = remote(masked_ref.at[1 - gy], own, own_sems.at[0], own_sems.at[1], mate)
-    own_copy.start()
+    for q in range(len(starts)):
+        same_copies[q].start()
+        cross_copies[q].start()
+        if q == 0:
+            for copy in geo_copies[1:]:
+                copy.start()
+            geo_copies[0].start()
+        own_copies[q].start()
 
     geo[gy, width:width + cells] = geo_ref[...]
     corr = corr_ref[...]
@@ -158,26 +162,13 @@
     low = (corr - high.astype(jnp.float32)).astype(jnp.bfloat16)
     weights = jnp.concatenate([high, high, low], axis=1)
 
-    own_copy.wait()
-    geo_copies[0].wait()
-    forward = []
-    for side, start in ((1, 0), (2, width + cells)):
-        geo_copies[side].wait()
-        forward.append(remote(
-            geo.at[gy, pl.ds(start, width)], geo.at[gy, pl.ds(start, width)],
-            geo_sems.at[0, 2 + side], geo_sems.at[1, 2 + side], mate))
-        forward[-1].start()
-
-    def send_halo(r, k):
-        copies = (
+    def halo_copies(r, k):
+        return (
             remote(field.at[k, pl.ds(width, width)], halo.at[r, 1, k],
                    halo_sems.at[0, r, 0, k], halo_sems.at[1, r, 0, k], west_dev),
             remote(field.at[k, pl.ds(cells, width)], halo.at[r, 0, k],
                    halo_sems.at[0, r, 1, k], halo_sems.at[1, r, 1, k], east_dev),
         )
-        for copy in copies:
-            copy.start()
-        return copies
 
     def vertical(x):
         mine = masked_ref[gy, x]
@@ -197,14 +188,25 @@
                 wet = geo[half, width + x, k * TILE:(k + 1) * TILE]
                 field[k, width + x, half] = value * wet
 
-    for place, q in enumerate(order):
-        same_copies[place].wait()
-        cross_copies[place].wait()
-        for x in range(q * part, (q + 1) * part):
+    pending = [halo_copies(0, k) for k in range(tiles)]
+    forward = []
+    geo_copies[0].wait()
+    for q, (start, size) in enumerate(starts):
+        own_copies[q].wait()
+        same_copies[q].wait()
+        cross_copies[q].wait()
+        for x in range(start, start + size):
             vertical(x)
-
-    pending = [send_halo(0, k) for k in range(tiles)]
-
+        if q < 2:
+            for k in range(tiles):
+                pending[k][q].start()
+        if q == 1:
+            for side, place in ((1, 0), (2, width + cells)):
+                geo_copies[side].wait()
+                edge = geo.at[gy, pl.ds(place, width)]
+                forward.append(remote(
+                    edge, edge, geo_sems.at[0, 2 + side], geo_sems.at[1, 2 + side], mate))
+                forward[-1].start()
     for copy in forward:
         copy.wait()
     for half in range(2):
@@ -251,7 +253,9 @@
                 copy.wait()
             relax_tile(r, k)
             if r < rounds - 1:
-                later.append(send_halo(r + 1, k))
+                later.append(halo_copies(r + 1, k))
+                for copy in later[-1]:
+                    copy.start()
             else:
                 out_copies.append(remote(
                     field.at[k, pl.ds(width, cells), 1 - gy], out_ref.at[gy, k],
@@ -298,9 +302,9 @@
             pltpu.VMEM((rounds, 2, tiles, width, 2, TILE, lanes), f32),
             pltpu.VMEM((rows, 2, TILE, lanes), f32),
             pltpu.VMEM((rows, 2, TILE, lanes), f32),
-            dma((2,)),
-            dma((2, PARTS)),
-            dma((2, PARTS)),
+            dma((2, 3)),
+            dma((2, 3)),
+            dma((2, 3)),
             dma((2, 5)),
             dma((2, rounds, 2, tiles)),
             dma((2, tiles)),

time: 47.7 us -> 40.2 us (0.84)
  Pallas kernels: 43.3 us -> 35.8 us
    pallas_call x1, Pallas kernels: 43.3 us -> 35.8 us  [fused(): pl.pallas_call(kernel, out_shape=jax.ShapeDtypeStruct((2, tiles, cells, T...]
where the time goes in v2:
time: 40.2 us; the launch traced here: 39.9 us
  Pallas kernels  35.8 us (89%)
  local copies, waits for them, and re-layouts  2.51 us (6%)
  other arithmetic  1.56 us (4%)
    pallas_call x1, Pallas kernels, fused(): pl.pallas_call(kernel, out_shape=jax.ShapeDtypeStruct((2, tiles, cells, T...  35.8 us
    convert_element_type x1, other arithmetic, fused(): (turned * (numbers[None, :, None] < level_count[:, None, :]).astype(jnp.i...  1.15 us
    transpose x1, local copies, waits for them, and re-layouts, fused(): return result.transpose(0, 1, 3, 2, 4).reshape(increments.shape)  0.95 us

profile of v2, /device:TPU:0, one launch (start us, length us, event | category | flops | bytes accessed | tf_op | source)
XLA Modules:
  0.0 39.9 jit_solution(9174130552760226308)
XLA Ops:
  0.0 0.0 copy-start.1
  0.0 0.1 pad.5.clone
  0.1 0.7 %fusion.2 = (f32[1,16,128]{2,1,0:T(8,128)S(1)}, f32[1,16,128]{2,1,0:T(8,128)S(1)}) fusion(f32[2,16,128]{2,1,0:T(8,128)} %param.7), kind=kLoop, calls=%fused_computation.10 | loop fusion | bytes 32768 | tf_op jit(solution)/shard_map/slice | solution.py:286
  0.8 0.1 copy-done.1
  0.9 0.1 fusion.1
  1.0 0.0 copy-start.2
  1.0 0.1 maximum_select_fusion.corr_ref
  1.0 0.6 %copy-done.2 = s32[16,128]{1,0:T(8,128)S(1)} copy-done((s32[16,128]{1,0:T(8,128)S(1)}, s32[16,128]{1,0:T(8,128)}, u32[]{:S(2)}) %copy-start.2) | copy-done | bytes 8216
  1.7 0.0 copy-start
  1.7 1.2 %fusion = f32[16,40,128]{2,1,0:T(8,128)S(1)} fusion(s32[40,16,128]{2,1,0:T(8,128)} %param.8, s32[16,128]{1,0:T(8,128)S(1)} %copy-done.2, s32[40]{0:T(128)S(1)} %iota_add_fusion), kind=kLoop, calls=%fused_computation.3 | loop fusion | flops 245760 | bytes 663712 | tf_op jit(solution)/shard_map/convert_element_type | solution.py:280
  2.8 0.1 maximum_maximum_fusion.geo_ref
  2.9 0.0 copy-done
  2.9 0.2 bitcast_multiply_fusion.masked_ref
  3.2 35.8 %shard_map.55 = f32[2,5,16,8,128]{4,3,2,1,0:T(8,128)S(1)} custom-call(f32[2,16,40,128]{3,2,1,0:T(8,128)S(1)} %bitcast_multiply_fusion.masked_ref, f32[16,48,128]{2,1,0:T(8,128)S(1)} %maximum_maximum_fusion.geo_ref, f32[40,80]{1,0:T(8,128)S(1)} %maximum_select_fusion.corr_ref), custom_call_target="tpu_custom_call" | custom-call | flops 60000000 | bytes 4000000 | tf_op jit(solution)/shard_map/pallas_call | solution.py:292
  38.9 1.0 %copy.10 = f32[2,5,8,16,128]{4,3,2,1,0:T(8,128)} copy(f32[2,5,8,16,128]{4,2,3,1,0:T(8,128)S(1)} %bitcast.16) | data formatting | bytes 1310720 | tf_op jit(solution)/shard_map/transpose | solution.py:317
  (5 shorter events, 0.0 us)
Async XLA Ops:
  0.0 0.9 %copy-start.1 = (f32[2,80,80]{2,1,0:T(8,128)S(1)}, f32[2,80,80]{2,1,0:T(8,128)}, u32[]{:S(2)}) copy-start(f32[2,80,80]{2,1,0:T(8,128)} %param.6) | copy-start | bytes 153604
  1.0 0.7 %copy-start.2 = (s32[16,128]{1,0:T(8,128)S(1)}, s32[16,128]{1,0:T(8,128)}, u32[]{:S(2)}) copy-start(s32[16,128]{1,0:T(8,128)} %param.9) | copy-start | bytes 24580
  1.7 1.3 %copy-start = (f32[1,2,40,16,128]{4,3,2,1,0:T(8,128)S(1)}, f32[1,2,40,16,128]{4,3,2,1,0:T(8,128)}, u32[]{:S(2)}) copy-start(f32[1,2,40,16,128]{4,3,2,1,0:T(8,128)} %param.5) | copy-start | bytes 1966084

commit v3 on v2

--- a/solution.py
+++ b/solution.py
@@ -102,7 +102,7 @@
 
 
 def kernel(
-    masked_ref, geo_ref, corr_ref, out_ref,
+    masked_ref, wet_ref, corr_ref, kappa_ref, out_ref,
     geo, own, other, field, halo, east, north,
     own_sems, same_sems, cross_sems, geo_sems, halo_sems, out_sems,
 ):
@@ -110,6 +110,7 @@
     count = lax.axis_size("gx")
     cells = masked_ref.shape[1]
     levels = masked_ref.shape[2]
+    lanes = masked_ref.shape[3]
     tiles = levels // TILE
     width = WIDTH
     rows = cells + 2 * width
@@ -124,6 +125,13 @@
     everyone = (east_dev, west_dev, mate, pair, cross)
     for device in everyone:
         pl.semaphore_signal(barrier, inc=1, device_id=device, device_id_type=MESH)
+    columns = gy * lanes + lax.broadcasted_iota(jnp.int32, (1, lanes), 1)
+    is_open = (columns != lanes * lax.axis_size("gy") - 1).astype(jnp.float32)
+    geo[gy, width:width + cells, 0:levels] = wet_ref[...]
+    for x in range(cells):
+        geo[gy, width + x, levels:levels + 1] = kappa_ref[0, x:x + 1]
+        geo[gy, width + x, levels + 1:levels + 2] = kappa_ref[1, x:x + 1] * is_open
+        geo[gy, width + x, levels + 2:] = jnp.zeros((TILE - 2, lanes), jnp.float32)
     pl.semaphore_wait(barrier, len(everyone))
 
     starts = ((0, width), (cells - width, width), (width, cells - 2 * width))
@@ -139,11 +147,11 @@
             masked_ref.at[1 - gy, span], other.at[gy, span],
             cross_sems.at[0, q], cross_sems.at[1, q], cross))
     geo_copies = [
-        remote(geo_ref, geo.at[gy, pl.ds(width, cells)], geo_sems.at[0, 0], geo_sems.at[1, 0], mate),
-        remote(geo_ref.at[pl.ds(cells - width, width)],
+        remote(geo.at[gy, pl.ds(width, cells)], geo.at[gy, pl.ds(width, cells)], geo_sems.at[0, 0], geo_sems.at[1, 0], mate),
+        remote(geo.at[gy, pl.ds(cells, width)],
                geo.at[gy, pl.ds(0, width)],
                geo_sems.at[0, 1], geo_sems.at[1, 1], east_dev),
-        remote(geo_ref.at[pl.ds(0, width)],
+        remote(geo.at[gy, pl.ds(width, width)],
                geo.at[gy, pl.ds(width + cells, width)],
                geo_sems.at[0, 2], geo_sems.at[1, 2], west_dev),
     ]
@@ -156,8 +164,9 @@
             geo_copies[0].start()
         own_copies[q].start()
 
-    geo[gy, width:width + cells] = geo_ref[...]
-    corr = corr_ref[...]
+    mine = corr_ref[gy, pl.ds(pl.multiple_of(lev * levels, TILE), levels), :]
+    swapped = jnp.concatenate([mine[:, levels:], mine[:, :levels]], axis=1)
+    corr = jnp.where(lev == 0, mine, swapped)
     high = corr.astype(jnp.bfloat16)
     low = (corr - high.astype(jnp.float32)).astype(jnp.bfloat16)
     weights = jnp.concatenate([high, high, low], axis=1)
@@ -273,26 +282,18 @@
     width = WIDTH
     rows = cells + 2 * width
     rounds = PASSES // width
-    gy = lax.axis_index("gy")
     lev = lax.axis_index("lev")
     numbers = lev * levels + jnp.arange(levels, dtype=jnp.int32)
     turned = jnp.swapaxes(sea_mask, 0, 1)
     wet = (turned * (numbers[None, :, None] < level_count[:, None, :]).astype(jnp.int32)).astype(jnp.float32)
     masked = jnp.swapaxes(increments[0], 1, 2) * wet[None]
-    total_y = lanes * lax.axis_size("gy")
-    local_rows = gy * lanes + jnp.arange(lanes, dtype=jnp.int32)
-    north = kappa[1] * (local_rows != total_y - 1).astype(jnp.float32)[None]
-    fill = jnp.zeros((cells, TILE - 2, lanes), jnp.float32)
-    geo = jnp.concatenate([wet, kappa[0][:, None], north[:, None], fill], axis=1)
-    mine = lax.dynamic_slice(vert_corr, (gy, lev * levels, 0), (1, levels, 2 * levels))[0]
-    corr = jnp.where(lev == 0, mine, jnp.roll(mine, levels, 1))
     vmem = pl.BlockSpec(memory_space=pltpu.VMEM)
     f32 = jnp.float32
     dma = pltpu.SemaphoreType.DMA
     result = pl.pallas_call(
         kernel,
         out_shape=jax.ShapeDtypeStruct((2, tiles, cells, TILE, lanes), f32),
-        in_specs=[vmem] * 3,
+        in_specs=[vmem] * 4,
         out_specs=vmem,
         scratch_shapes=[
             pltpu.VMEM((2, rows, levels + TILE, lanes), f32),
@@ -313,7 +314,7 @@
             collective_id=0, has_side_effects=True, vmem_limit_bytes=32 * 1024 * 1024
         ),
         cost_estimate=pl.CostEstimate(flops=60_000_000, bytes_accessed=4_000_000, transcendentals=0),
-    )(masked, geo, corr)
+    )(masked, wet, vert_corr, kappa)
     return result.transpose(0, 1, 3, 2, 4).reshape(increments.shape)
 
 

time: 40.2 us -> 39.5 us (0.983)
    slice x2 -> x0, local copies, waits for them, and re-layouts: 0.79 us -> none  [the longest x1 0.72 us: fused(): kappa[0][:, None]]
    unnamed x6 -> x8, local copies, waits for them, and re-layouts: 0.69 us -> 1.35 us
where the time goes in v3:
time: 39.5 us; the launch traced here: 39.4 us
  Pallas kernels  35.7 us (90%)
  local copies, waits for them, and re-layouts  2.3 us (6%)
  other arithmetic  1.3 us (3%)
    pallas_call x1, Pallas kernels, fused(): pl.pallas_call(kernel, out_shape=jax.ShapeDtypeStruct((2, tiles, cells, T...  35.7 us
    unnamed x8, local copies, waits for them, and re-layouts  1.35 us
    convert_element_type x1, other arithmetic, fused(): (turned * (numbers[None, :, None] < level_count[:, None, :]).astype(jnp.i...  1.08 us
    transpose x1, local copies, waits for them, and re-layouts, fused(): return result.transpose(0, 1, 3, 2, 4).reshape(increments.shape)  0.95 us

profile of v3, /device:TPU:0, one launch (start us, length us, event | category | flops | bytes accessed | tf_op | source)
XLA Modules:
  0.0 39.4 jit_solution(15106805755381152222)
XLA Ops:
  0.0 0.0 copy-start.3
  0.0 0.0 copy-start.2
  0.0 0.7 %copy-done.3 = s32[16,128]{1,0:T(8,128)S(1)} copy-done((s32[16,128]{1,0:T(8,128)S(1)}, s32[16,128]{1,0:T(8,128)}, u32[]{:S(2)}) %copy-start.3) | copy-done | bytes 8216
  0.7 1.1 %fusion.wet_ref = f32[16,40,128]{2,1,0:T(8,128)S(1)} fusion(s32[40,16,128]{2,1,0:T(8,128)} %param.8, s32[16,128]{1,0:T(8,128)S(1)} %copy-done.3, s32[40]{0:T(128)S(1)} %iota_add_fusion), kind=kLoop, calls=%fused_computation.2 | loop fusion | flops 245760 | bytes 663712 | tf_op jit(solution)/shard_map/convert_element_type | solution.py:288
  1.8 0.0 copy-done.2
  1.8 0.0 copy-start
  1.8 0.0 copy-start.1
  1.8 0.2 bitcast_multiply_fusion.masked_ref
  2.0 0.6 %copy-done = f32[2,80,80]{2,1,0:T(8,128)S(1)} copy-done((f32[2,80,80]{2,1,0:T(8,128)S(1)}, f32[2,80,80]{2,1,0:T(8,128)}, u32[]{:S(2)}) %copy-start) | copy-done | bytes 51224
  2.7 0.0 copy-done.1
  2.7 35.7 %shard_map.55 = f32[2,5,16,8,128]{4,3,2,1,0:T(8,128)S(1)} custom-call(f32[2,16,40,128]{3,2,1,0:T(8,128)S(1)} %bitcast_multiply_fusion.masked_ref, f32[16,40,128]{2,1,0:T(8,128)S(1)} %fusion.wet_ref, f32[2,80,80]{2,1,0:T(8,128)S(1)} %copy-done, f32[2,16,128]{2,1,0:T(8,128)S(1)} %copy-done.1), custom_call_target="tpu_custom_call" | custom-call | flops 60000000 | bytes 4000000 | tf_op jit(solution)/shard_map/pallas_call | solution.py:293
  38.4 1.0 %copy.10 = f32[2,5,8,16,128]{4,3,2,1,0:T(8,128)} copy(f32[2,5,8,16,128]{4,2,3,1,0:T(8,128)S(1)} %bitcast.10) | data formatting | bytes 1310720 | tf_op jit(solution)/shard_map/transpose | solution.py:318
  (1 shorter events, 0.0 us)
Async XLA Ops:
  0.0 0.7 %copy-start.3 = (s32[16,128]{1,0:T(8,128)S(1)}, s32[16,128]{1,0:T(8,128)}, u32[]{:S(2)}) copy-start(s32[16,128]{1,0:T(8,128)} %param.9) | copy-start | bytes 24580
  0.0 1.8 %copy-start.2 = (f32[1,2,40,16,128]{4,3,2,1,0:T(8,128)S(1)}, f32[1,2,40,16,128]{4,3,2,1,0:T(8,128)}, u32[]{:S(2)}) copy-start(f32[1,2,40,16,128]{4,3,2,1,0:T(8,128)} %param.5) | copy-start | bytes 1966084
  1.8 0.9 %copy-start = (f32[2,80,80]{2,1,0:T(8,128)S(1)}, f32[2,80,80]{2,1,0:T(8,128)}, u32[]{:S(2)}) copy-start(f32[2,80,80]{2,1,0:T(8,128)} %corr_ref.1) | copy-start | bytes 153604
  1.8 0.9 %copy-start.1 = (f32[2,16,128]{2,1,0:T(8,128)S(1)}, f32[2,16,128]{2,1,0:T(8,128)}, u32[]{:S(2)}) copy-start(f32[2,16,128]{2,1,0:T(8,128)} %kappa_ref.1) | copy-start | bytes 49156
